TPU v7x, 32 devices: a whole 2x2x4 slice. The times are simulated.
32 devices in a mesh: vir: 8 (over z, x), occ: 4 (over y, core).
Axes of the slice: x: 2, y: 2, z: 4, core: 2. Of those that a mesh axis runs over, the one named last changes fastest.
Arguments:
- integrals: bfloat16 [1024, 1024], P(None, 'vir'), as said below
- amplitudes: bfloat16 [1024, 256], P('vir', 'occ'), may hold values from -6 to 6
- labels: int32 [8], replicated, may hold values from 0 to 7
Outputs:
- residual: bfloat16 [1024, 256], P('vir', 'occ')
Inputs may be any that keep to these rules, and one draw needn't show every extreme that they name: integrals is symmetric: integrals[x, y] == integrals[y, x].
All inputs are finite; a program needn't handle non-finite values.
Results may differ from a plain program's by a relative error of at most 0.001.
Values may be sent and summed in bfloat16 or wider, within the bound.
A program may use at most 64 MiB of HBM per device.

v0:
```python
import functools
import math

import jax
import jax.numpy as jnp
from jax import lax
from jax.experimental import pallas as pl
from jax.experimental.pallas import tpu as pltpu
from jax.sharding import PartitionSpec as P

MESH = pl.DeviceIdType.MESH
UNROLL_UP_TO = 64


def repeat(low, high, body):
    if high - low <= UNROLL_UP_TO:
        for step in range(low, high):
            body(step)
    else:
        lax.fori_loop(low, high, lambda step, carry: (body(step), carry)[1], 0)


def kernel(outer, inner, owners, q, labels_hbm, integrals_hbm, amplitudes_hbm, out_ref,
           gathered, integrals, wide, labels, load_sem, send_sem, recv_sem):
    cols, width = amplitudes_hbm.shape
    nocc, piece, tiles = q * owners, q * q, outer * inner
    me, own = lax.axis_index("vir"), lax.axis_index("occ")
    far, near = me // inner, lax.rem(me, inner)
    way = 1 - 2 * (far // max(outer // 2, 1))

    def peer(step):
        return (lax.rem(far + way * (step // (inner * owners)) + outer, outer) * inner
                + lax.rem(near + step // owners % inner, inner),
                lax.rem(own + step % owners, owners))

    def held(tile, start, rows):
        return gathered.at[pl.ds(pl.multiple_of(tile * 2 * cols + start, piece), rows)]

    barrier = pltpu.get_barrier_semaphore()
    load_amplitudes = pltpu.make_async_copy(amplitudes_hbm, integrals.at[pl.ds(tiles * width, cols)],
                                            load_sem.at[0])
    load_integrals = pltpu.make_async_copy(integrals_hbm, integrals.at[pl.ds(0, tiles * width)],
                                           load_sem.at[1])
    load_labels = pltpu.make_async_copy(labels_hbm, labels, load_sem.at[2])
    load_amplitudes.start()
    load_labels.start()
    load_integrals.start()
    repeat(1, tiles * owners, lambda step: pl.semaphore_signal(
        barrier, inc=1, device_id=peer(step), device_id_type=MESH))

    load_amplitudes.wait()
    wide[pl.ds(0, cols)] = integrals[pl.ds(tiles * width, cols)].astype(jnp.float32)
    for owner in range(owners):
        for first in range(q):
            wide[pl.ds(cols + owner * piece + first * q, q)] = (
                wide[pl.ds(first * nocc + owner * q, q)])
    own_rows = pl.multiple_of(me * 2 * cols, piece)
    gathered[pl.ds(own_rows, cols)] = wide[pl.ds(cols, cols)].astype(jnp.bfloat16)

    def clear(tile):
        rows = pl.ds(pl.multiple_of(tile * 2 * cols + cols + own * piece, piece), piece)
        gathered[rows] = jnp.zeros((piece, width), jnp.bfloat16)

    repeat(0, tiles, clear)

    pl.semaphore_wait(barrier, tiles * owners - 1)

    def send(tile):
        def copy(source, target, owner):
            pltpu.make_async_remote_copy(
                src_ref=source, dst_ref=target, send_sem=send_sem.at[0],
                recv_sem=recv_sem.at[me], device_id=(tile, owner), device_id_type=MESH).start()

        @pl.when(tile != me)
        def _():
            copy(held(me, 0, cols), held(me, 0, cols), own)

        for step in range(1, owners):
            owner = lax.rem(own + step, owners)
            copy(held(me, owner * piece, piece), held(me, cols + own * piece, piece), owner)

    repeat(0, tiles, send)

    def arrived(rows, semaphore):
        some = gathered.at[pl.ds(0, rows)]
        pltpu.make_async_copy(some, some, semaphore).wait()

    load_labels.wait()
    load_integrals.wait()

    def mask(tile):
        same = (labels[tile] == labels[me]).astype(jnp.float32)
        weight = jnp.full((width, width), same, jnp.float32).astype(jnp.bfloat16)
        rows = pl.ds(tile * width, width)
        integrals[rows] = integrals[rows] * weight

    repeat(0, tiles, mask)

    def add(step, total):
        tile = peer(step * owners)[0]
        arrived(cols - piece if isinstance(step, int) and step == 0 else 2 * cols - piece,
                recv_sem.at[tile])
        return total + jnp.dot(
            gathered[pl.ds(pl.multiple_of(tile * 2 * cols, piece), 2 * cols)],
            integrals[pl.ds(pl.multiple_of(tile * width, width), width)],
            preferred_element_type=jnp.float32)

    total = add(0, jnp.zeros((2 * cols, width), jnp.float32))
    if tiles <= UNROLL_UP_TO:
        for step in range(1, tiles):
            total = add(step, total)
    else:
        total = lax.fori_loop(1, tiles, add, total)

    wide[...] = total
    share = pl.multiple_of(own * piece, piece)
    wide[pl.ds(cols + share, piece)] = wide[pl.ds(share, piece)]
    for first in range(q):
        ladder = jnp.concatenate(
            [wide[pl.ds(owner * piece + first * q, q)] for owner in range(owners)], axis=0)
        mirrored = wide[pl.ds(cols + first, nocc, stride=q)]
        out_ref[pl.ds(first * nocc, nocc)] = (0.5 * (ladder - mirrored)).astype(jnp.bfloat16)

    arrived((tiles - 1) * cols + tiles * (cols - piece), send_sem.at[0])


def per_device(integrals, amplitudes, labels):
    width, cols = amplitudes.shape
    tiles, owners = lax.axis_size("vir"), lax.axis_size("occ")
    q = math.isqrt(cols // owners)
    inner = 1 if tiles % 2 else 2
    outer = tiles // inner
    anywhere = pl.BlockSpec(memory_space=pltpu.HBM)
    flipped = pl.pallas_call(
        functools.partial(kernel, outer, inner, owners, q),
        out_shape=jax.ShapeDtypeStruct((cols, width), jnp.bfloat16),
        in_specs=[anywhere] * 3,
        out_specs=pl.BlockSpec(memory_space=pltpu.VMEM),
        scratch_shapes=[
            pltpu.VMEM((tiles * 2 * cols, width), jnp.bfloat16),
            pltpu.VMEM((tiles * width + cols, width), jnp.bfloat16),
            pltpu.VMEM((2 * cols, width), jnp.float32),
            pltpu.SMEM(labels.shape, jnp.int32),
            pltpu.SemaphoreType.DMA((3,)),
            pltpu.SemaphoreType.DMA((1,)),
            pltpu.SemaphoreType.DMA((tiles,)),
        ],
        compiler_params=pltpu.CompilerParams(
            collective_id=0, has_side_effects=True, vmem_limit_bytes=32 << 20),
        cost_estimate=pl.CostEstimate(
            flops=4 * tiles * width * width * cols,
            bytes_accessed=2 * tiles * width * (width + 2 * cols), transcendentals=0),
    )(*(pltpu.with_memory_space_constraint(a, pltpu.HBM) for a in (labels, integrals, amplitudes.T)))
    return flipped.T


def solution(mesh):
    placed = (P(None, "vir"), P("vir", "occ"), P())
    return jax.shard_map(
        per_device, mesh=mesh, in_specs=placed, out_specs=P("vir", "occ"), check_vma=False
    )
```

profile of v0, /device:TPU:0, one launch (start us, length us, event | category | flops | bytes accessed | tf_op | source)
XLA Modules:
  0.0 12.6 jit_solution(11045526700683088734)
XLA Ops:
  0.0 12.0 %shard_map.37 = bf16[64,128]{1,0:T(8,128)(2,1)S(1)} custom-call(s32[8]{0:T(128)} %labels_hbm.1, bf16[1024,128]{1,0:T(8,128)(2,1)} %integrals_hbm.1, bf16[64,128]{1,0:T(8,128)(2,1)} %bitcast.3), custom_call_target="tpu_custom_call" | custom-call | flops 33554432 | bytes 524288 | tf_op jit(solution)/shard_map/pallas_call | solution.py:134
  12.0 0.6 %copy.5 = bf16[128,64]{0,1:T(8,128)(2,1)} copy(bf16[128,64]{0,1:T(8,128)(2,1)S(1)} %bitcast.2) | data formatting | bytes 32768
where the time goes:
time: 12.9 us; the launch traced here: 12.6 us
  Pallas kernels  12 us (93%)
  local copies, waits for them, and re-layouts  0.61 us (5%)
    pallas_call x1, Pallas kernels, per_device(): pl.pallas_call(functools.partial(kernel, outer, inner, owners, q), out_sh...  12 us
    unnamed x1, local copies, waits for them, and re-layouts  0.61 us

commit v1 on v0

--- a/solution.py
+++ b/solution.py
@@ -71,13 +71,14 @@
                 src_ref=source, dst_ref=target, send_sem=send_sem.at[0],
                 recv_sem=recv_sem.at[me], device_id=(tile, owner), device_id_type=MESH).start()
 
-        @pl.when(tile != me)
-        def _():
-            copy(held(me, 0, cols), held(me, 0, cols), own)
+        for owner in range(owners):
+            @pl.when((owner == own) & (tile != me))
+            def _():
+                copy(held(me, 0, cols), held(me, 0, cols), owner)
 
-        for step in range(1, owners):
-            owner = lax.rem(own + step, owners)
-            copy(held(me, owner * piece, piece), held(me, cols + own * piece, piece), owner)
+            @pl.when(owner != own)
+            def _():
+                copy(held(me, owner * piece, piece), held(me, cols + own * piece, piece), owner)
 
     repeat(0, tiles, send)
 

time: 12.9 us -> 12.6 us (0.977)
  Pallas kernels: 12 us -> 11.8 us
    pallas_call x1, Pallas kernels: 12 us -> 11.8 us  [per_device(): pl.pallas_call(functools.partial(kernel, outer, inner, owners, q), out_sh...]
where the time goes in v1:
time: 12.6 us; the launch traced here: 12.4 us
  Pallas kernels  11.8 us (94%)
  local copies, waits for them, and re-layouts  0.61 us (5%)
    pallas_call x1, Pallas kernels, per_device(): pl.pallas_call(functools.partial(kernel, outer, inner, owners, q), out_sh...  11.8 us
    unnamed x1, local copies, waits for them, and re-layouts  0.61 us

profile of v1, /device:TPU:0, one launch (start us, length us, event | category | flops | bytes accessed | tf_op | source)
XLA Modules:
  0.0 12.4 jit_solution(15738255291643478130)
XLA Ops:
  0.0 11.8 %shard_map.37 = bf16[64,128]{1,0:T(8,128)(2,1)S(1)} custom-call(s32[8]{0:T(128)} %labels_hbm.1, bf16[1024,128]{1,0:T(8,128)(2,1)} %integrals_hbm.1, bf16[64,128]{1,0:T(8,128)(2,1)} %bitcast.3), custom_call_target="tpu_custom_call" | custom-call | flops 33554432 | bytes 524288 | tf_op jit(solution)/shard_map/pallas_call | solution.py:135
  11.8 0.6 %copy.5 = bf16[128,64]{0,1:T(8,128)(2,1)} copy(bf16[128,64]{0,1:T(8,128)(2,1)S(1)} %bitcast.2) | data formatting | bytes 32768

commit v2 on v1

--- a/solution.py
+++ b/solution.py
@@ -46,7 +46,7 @@
     load_labels.start()
     load_integrals.start()
     repeat(1, tiles * owners, lambda step: pl.semaphore_signal(
-        barrier, inc=1, device_id=peer(step), device_id_type=MESH))
+        barrier, inc=1, device_id=peer(tiles * owners - step), device_id_type=MESH))
 
     load_amplitudes.wait()
     wide[pl.ds(0, cols)] = integrals[pl.ds(tiles * width, cols)].astype(jnp.float32)

time: 12.6 us -> 12.6 us (level)
  no operation moved by 1% of the time
where the time goes in v2:
time: 12.6 us; the launch traced here: 12.3 us
  Pallas kernels  11.7 us (93%)
  local copies, waits for them, and re-layouts  0.61 us (5%)
    pallas_call x1, Pallas kernels, per_device(): pl.pallas_call(functools.partial(kernel, outer, inner, owners, q), out_sh...  11.7 us
    unnamed x1, local copies, waits for them, and re-layouts  0.61 us

profile of v2, /device:TPU:0, one launch (start us, length us, event | category | flops | bytes accessed | tf_op | source)
XLA Modules:
  0.0 12.3 jit_solution(3783299025407478884)
XLA Ops:
  0.0 11.7 %shard_map.37 = bf16[64,128]{1,0:T(8,128)(2,1)S(1)} custom-call(s32[8]{0:T(128)} %labels_hbm.1, bf16[1024,128]{1,0:T(8,128)(2,1)} %integrals_hbm.1, bf16[64,128]{1,0:T(8,128)(2,1)} %bitcast.3), custom_call_target="tpu_custom_call" | custom-call | flops 33554432 | bytes 524288 | tf_op jit(solution)/shard_map/pallas_call | solution.py:135
  11.7 0.6 %copy.5 = bf16[128,64]{0,1:T(8,128)(2,1)} copy(bf16[128,64]{0,1:T(8,128)(2,1)S(1)} %bitcast.2) | data formatting | bytes 32768
